TPU v7x, 32 devices: a whole 2x2x4 slice. The times are simulated.
32 devices in a mesh: tm: 8 (over z, y), panel: 4 (over x, core).
Axes of the slice: x: 2, y: 2, z: 4, core: 2. Of those that a mesh axis runs over, the one named last changes fastest.
Arguments:
- transitions: float32 [16, 1024, 1024], P('tm', None, 'panel'), may hold values from 0 to 1, as said below
- start_weights: float32 [1024], replicated, may hold values from 0.1 to 10
Outputs:
- window_kernel: float32 [8, 1024, 1024], P('tm', None, 'panel')
- occupancy: float32 [8, 1024], P('tm', 'panel')
Inputs may be any that keep to these rules, and one draw needn't show every extreme that they name: `transitions`: every entry is nonnegative; each diagonal entry is 0.3 or more; each row sums to between 0.3 and 1.7.
All inputs are finite; a program needn't handle non-finite values.
Results may differ from a plain program's by a relative error of at most 0.0003.
Values sent between devices are 32-bit elements; how exact they have to be, the bound alone decides.
A program may use at most 64 MiB of HBM per device.

v0:
```python
import jax
import jax.numpy as jnp
from jax import lax
from jax.sharding import PartitionSpec as P

LEVELS = 2


def passed_along(array, axis, by):
    size = lax.axis_size(axis)
    pairs = [(i, i + by) for i in range(size) if 0 <= i + by < size]
    return lax.ppermute(array, axis, pairs)


def matmul_high(left, right):
    return jnp.dot(left, right, precision=lax.Precision.HIGHEST, preferred_element_type=jnp.float32)


def make_adder(right, piece):
    return matmul_high(piece, right)


def body(transitions, start_weights):
    states = transitions.shape[1]
    position = lax.axis_index("tm")
    current = transitions[0]
    current = make_adder(transitions[1], lax.all_gather(current, "panel", axis=1, tiled=True))
    for level in range(LEVELS):
        reach = 2**level
        earlier = passed_along(current, "tm", reach)
        joined = make_adder(current, lax.all_gather(earlier, "panel", axis=1, tiled=True))
        current = jnp.where(position >= reach, joined, current)
    window_kernel = (current * jnp.float32(states))[None]
    occupancy = matmul_high(start_weights[None, :], current)
    return (window_kernel, occupancy)


def solution(mesh):
    placed = (P("tm", None, "panel"), P())
    return jax.shard_map(
        body,
        mesh=mesh,
        in_specs=placed,
        out_specs=(P("tm", None, "panel"), P("tm", "panel")),
        check_vma=False,
    )
```

profile of v0, /device:TPU:13, one launch (start us, length us, event | category | flops | bytes accessed | tf_op | source)
XLA Modules:
  0.0 196.7 jit_solution(6509264082568385762)
XLA Ops:
  7.2 0.0 copy-start
  7.2 0.0 all-gather.9.cloned.1.call-start
  7.2 2.3 %slice.6 = f32[1,1024,256]{2,1,0:T(8,128)} slice(f32[2,1024,256]{2,1,0:T(8,128)} %param.2), slice={[0:1], [0:1024], [0:256]} | slice | bytes 2097152 | tf_op jit(solution)/shard_map/slice | solution.py:26
  9.5 0.0 all-gather.9.cloned.1.call-update
  9.5 0.0 all-gather.5.cloned.1.call-start
  9.6 36.6 %all-gather.9.cloned.1.call-done = f32[1,1024,1024]{2,1,0:T(8,128)} async-done(((f32[1,1024,256]{2,1,0:T(8,128)}), f32[1,1024,1024]{2,1,0:T(8,128)}) %all-gather.9.cloned.1.call-update) | async-done | bytes 4194320 | tf_op jit(solution)/shard_map/all_gather | solution.py:27
  46.2 5.5 %fusion = f32[1024,256]{1,0:T(8,128)S(1)} fusion(f32[1,1024,1024]{2,1,0:T(8,128)} %all-gather.9.cloned.1.call-done, f32[2,1024,256]{2,1,0:T(8,128)} %param.2), kind=kOutput, calls=%fused_computation | convolution fusion | flops 3221225472 | bytes 6291456 | tf_op jit(solution)/shard_map/dot_general | solution.py:16
  51.7 3.1 %collective-permute-start = (f32[1024,256]{1,0:T(8,128)S(1)}, f32[1024,256]{1,0:T(8,128)S(1)}, u32[]{:S(2)}, u32[]{:S(2)}) collective-permute-start(f32[1024,256]{1,0:T(8,128)S(1)} %fusion), channel_id=1, source_target_pairs={{0,4},{4,8},{8,12},{12,16},{16,20},{20,24},{24,28},{1,5},{5,9},{9,... | collective-permute-start | bytes 3145736 | tf_op jit(solution)/shard_map/ppermute | solution.py:12
  54.8 23.3 %collective-permute-done = f32[1024,256]{1,0:T(8,128)S(1)} collective-permute-done((f32[1024,256]{1,0:T(8,128)S(1)}, f32[1024,256]{1,0:T(8,128)S(1)}, u32[]{:S(2)}, u32[]{:S(2)}) %collective-permute-start) | collective-permute-done | bytes 1048608 | tf_op jit(solution)/shard_map/ppermute | solution.py:12
  78.1 0.0 copy-start.1
  78.1 1.0 copy-done.1
  79.1 0.0 all-gather.5.cloned.1.call-update
  79.1 0.0 all-gather.7.cloned.1.call-start
  79.1 35.4 %all-gather.5.cloned.1.call-done = f32[1024,1024]{1,0:T(8,128)} async-done(((f32[1024,256]{1,0:T(8,128)}), f32[1024,1024]{1,0:T(8,128)}) %all-gather.5.cloned.1.call-update) | async-done | bytes 4194320 | tf_op jit(solution)/shard_map/all_gather | solution.py:31
  114.5 5.2 %convolution_select_fusion.1 = f32[1024,256]{1,0:T(8,128)S(1)} fusion(f32[1024,256]{1,0:T(8,128)S(1)} %fusion, f32[1024,1024]{1,0:T(8,128)} %all-gather.5.cloned.1.call-done, pred[]{:T(512)S(6)} %ge.7), kind=kOutput, calls=%fused_computation.3 | convolution fusion | flops 3221487616 | bytes 6291457 | tf_op jit(solution)/shard_map/dot_general | solution.py:16
  119.8 3.1 %collective-permute-start.1 = (f32[1024,256]{1,0:T(8,128)S(1)}, f32[1024,256]{1,0:T(8,128)S(1)}, u32[]{:S(2)}, u32[]{:S(2)}) collective-permute-start(f32[1024,256]{1,0:T(8,128)S(1)} %convolution_select_fusion.1), channel_id=1, source_target_pairs={{0,8},{4,12},{8,16},{12,20},{16,24},{20,28},{1,9},{5,13},{9,17},{1... | collective-permute-start | bytes 3145736 | tf_op jit(solution)/shard_map/ppermute | solution.py:12
  122.9 23.3 %collective-permute-done.1 = f32[1024,256]{1,0:T(8,128)S(1)} collective-permute-done((f32[1024,256]{1,0:T(8,128)S(1)}, f32[1024,256]{1,0:T(8,128)S(1)}, u32[]{:S(2)}, u32[]{:S(2)}) %collective-permute-start.1) | collective-permute-done | bytes 1048608 | tf_op jit(solution)/shard_map/ppermute | solution.py:12
  146.2 0.0 copy-start.2
  146.2 1.0 copy-done.2
  147.1 0.0 all-gather.7.cloned.1.call-update
  147.2 35.5 %all-gather.7.cloned.1.call-done = f32[1024,1024]{1,0:T(8,128)} async-done(((f32[1024,256]{1,0:T(8,128)}), f32[1024,1024]{1,0:T(8,128)}) %all-gather.7.cloned.1.call-update) | async-done | bytes 4194320 | tf_op jit(solution)/shard_map/all_gather | solution.py:31
  182.6 5.3 %convolution_select_fusion = f32[1024,256]{1,0:T(8,128)S(1)} fusion(f32[1024,256]{1,0:T(8,128)S(1)} %convolution_select_fusion.1, f32[1024,1024]{1,0:T(8,128)} %all-gather.7.cloned.1.call-done, pred[]{:T(512)S(6)} %ge.6), kind=kOutput, calls=%fused_computation.2 | convolution fusion | flops 3221487616 | bytes 6291457 | tf_op jit(solution)/shard_map/dot_general | solution.py:16
  187.9 1.0 multiply_bitcast_fusion
  189.0 0.0 copy-done
  189.0 1.2 fusion.4
Async XLA Ops:
  7.2 181.8 %copy-start = (f32[1024]{0:T(1024)S(1)}, f32[1024]{0:T(1024)}, u32[]{:S(2)}) copy-start(f32[1024]{0:T(1024)} %param.3) | copy-start | bytes 12292
  7.2 39.0 %all-gather.9.cloned.1.call-start = ((), (), s32[]{:S(2)}) async-start(), calls=%async_computation.2 | async-start | bytes 5242880 | tf_op jit(solution)/shard_map/all_gather | solution.py:27
  9.5 105.0 %all-gather.5.cloned.1.call-start = ((), (), s32[]{:S(2)}) async-start(), calls=%async_computation | async-start | bytes 5242880 | tf_op jit(solution)/shard_map/all_gather | solution.py:31
  51.7 26.4 %collective-permute-start = (f32[1024,256]{1,0:T(8,128)S(1)}, f32[1024,256]{1,0:T(8,128)S(1)}, u32[]{:S(2)}, u32[]{:S(2)}) collective-permute-start(f32[1024,256]{1,0:T(8,128)S(1)} %fusion), channel_id=1, source_target_pairs={{0,4},{4,8},{8,12},{12,16},{16,20},{20,24},{24,28},{1,5},{5,9},{9,... | collective-permute-start | bytes 3145736 | tf_op jit(solution)/shard_map/ppermute | solution.py:12
  78.1 1.0 copy-start.1
  79.1 103.6 %all-gather.7.cloned.1.call-start = ((), (), s32[]{:S(2)}) async-start(), calls=%async_computation.1 | async-start | bytes 5242880 | tf_op jit(solution)/shard_map/all_gather | solution.py:31
  119.8 26.4 %collective-permute-start.1 = (f32[1024,256]{1,0:T(8,128)S(1)}, f32[1024,256]{1,0:T(8,128)S(1)}, u32[]{:S(2)}, u32[]{:S(2)}) collective-permute-start(f32[1024,256]{1,0:T(8,128)S(1)} %convolution_select_fusion.1), channel_id=1, source_target_pairs={{0,8},{4,12},{8,16},{12,20},{16,24},{20,28},{1,9},{5,13},{9,17},{1... | collective-permute-start | bytes 3145736 | tf_op jit(solution)/shard_map/ppermute | solution.py:12
  146.2 1.0 copy-start.2
Sparse Core Ops, SparseCore 0:
  10.1 35.9 all-gather.8
  79.2 35.2 all-gather.4
  147.3 35.2 all-gather.6
where the time goes:
time: 198 us; the launch traced here: 197 us
  waiting for transfers between devices  154 us (78%)
  matrix products  17.2 us (9%)
  between operations  13.8 us (7%)
  starting transfers between devices  6.33 us (3%)
  local copies, waits for them, and re-layouts  4.21 us (2%)
    all_gather x2, waiting for transfers between devices, body(): lax.all_gather(earlier, 'panel', axis=1, tiled=True)  70.9 us
    ppermute x2, waiting for transfers between devices, passed_along(): return lax.ppermute(array, axis, pairs)  46.6 us
    all_gather x1, waiting for transfers between devices, body(): lax.all_gather(current, 'panel', axis=1, tiled=True)  36.6 us
    dot_general x4, matrix products, matmul_high(): jnp.dot(left, right, precision=lax.Precision.HIGHEST, preferred_element_t...  17.2 us
    ppermute x2, starting transfers between devices, passed_along(): return lax.ppermute(array, axis, pairs)  6.21 us
  transfers between devices with their start and end apart: 5, of which 5 were waited for; matrix products, arithmetic and copies ran while one was open for 0% of the time, Pallas kernels for 0%

commit v1 on v0

v1 whole, which is shorter than its diff:
```python
import functools

import jax
import jax.numpy as jnp
from jax import lax
from jax.experimental import pallas as pl
from jax.experimental.pallas import tpu as pltpu
from jax.sharding import PartitionSpec as P

LEVELS = 2
CHUNKS = 8
MESH = pl.DeviceIdType.MESH
HI = jnp.bfloat16


def split(value):
    high = value.astype(HI)
    return high, (value - high.astype(jnp.float32)).astype(HI)


def kernel(n_tm, n_panel, steps_ref, weights_ref, window_ref, occ_ref,
           full, right_f32, right_hi, right_lo,
           lo_send, lo_recv, hi_send, hi_recv, rel_send, rel_recv, tm_send, tm_recv):
    states, width = steps_ref.shape[1:]
    rows = states // CHUNKS
    halves = n_panel // 2
    t = lax.axis_index("tm")
    p = lax.axis_index("panel")
    hi, lo = p // 2, p % 2
    partner = hi * 2 + (1 - lo)

    def other(k):
        return lax.rem(hi + k, halves) * 2 + lo

    def back(k):
        return lax.rem(hi + halves - k, halves) * 2 + lo

    barrier = pltpu.get_barrier_semaphore()
    pl.semaphore_signal(barrier, inc=1, device_id={"panel": partner}, device_id_type=MESH)
    for k in range(1, halves):
        pl.semaphore_signal(barrier, inc=1, device_id={"panel": other(k)}, device_id_type=MESH)
    reaches = [2**level for level in range(LEVELS)]
    for reach in reaches:
        @pl.when(t + reach < n_tm)
        def _():
            pl.semaphore_signal(barrier, inc=1, device_id={"tm": t + reach}, device_id_type=MESH)

        @pl.when(t >= reach)
        def _():
            pl.semaphore_signal(barrier, inc=1, device_id={"tm": t - reach}, device_id_type=MESH)
    peers = halves
    for reach in reaches:
        peers += (t + reach < n_tm).astype(jnp.int32) + (t >= reach).astype(jnp.int32)
    pl.semaphore_wait(barrier, peers)

    def band(r):
        return pl.ds(pl.multiple_of(r * rows, rows), rows)

    def own(stage, r):
        return steps_ref.at[0, band(r)] if stage == 0 else full.at[stage, p, band(r)]

    def to_partner(stage, r):
        return pltpu.make_async_remote_copy(
            own(stage, r), full.at[stage, p, band(r)],
            lo_send.at[stage, r], lo_recv.at[stage, r],
            device_id={"panel": partner}, device_id_type=MESH)

    def to_other(stage, r, k):
        return pltpu.make_async_remote_copy(
            own(stage, r), full.at[stage, p, band(r)],
            hi_send.at[stage, k - 1, r], hi_recv.at[stage, k - 1, r],
            device_id={"panel": other(k)}, device_id_type=MESH)

    def relayed(stage, r, k):
        slot = full.at[stage, back(k), band(r)]
        return pltpu.make_async_remote_copy(
            slot, slot, rel_send.at[stage, k - 1, r], rel_recv.at[stage, k - 1, r],
            device_id={"panel": partner}, device_id_type=MESH)

    def along(stage, r):
        reach = reaches[stage]
        return pltpu.make_async_remote_copy(
            right_f32.at[stage, band(r)], full.at[stage + 1, p, band(r)],
            tm_send.at[stage, r], tm_recv.at[stage, r],
            device_id={"tm": t + reach}, device_id_type=MESH)

    def forward(stage, r):
        if stage:
            along(stage - 1, r).wait_recv()
        for k in range(1, halves):
            to_other(stage, r, k).start()
        to_partner(stage, r).start()

    def relay(stage, r):
        for k in range(1, halves):
            to_other(stage, r, k).wait_recv()
            relayed(stage, r, k).start()

    def product(stage, r):
        to_partner(stage, r).wait_recv()
        for k in range(1, halves):
            relayed(stage, r, k).wait_recv()
        total = jnp.zeros((rows, width), jnp.float32)
        for k in range(n_panel):
            a_hi, a_lo = split(full[stage, k, band(r), :])
            cols = pl.ds(k * width, width)
            b_hi, b_lo = right_hi[stage, cols, :], right_lo[stage, cols, :]
            both = jnp.dot(jnp.concatenate([a_hi, a_lo], axis=0), b_hi,
                           preferred_element_type=jnp.float32)
            total += both[:rows] + both[rows:] + jnp.dot(
                a_hi, b_lo, preferred_element_type=jnp.float32)
        return total

    def put(stage, r, value):
        if stage < LEVELS:
            right_f32[stage, band(r), :] = value
            high, low = split(value)
            right_hi[stage + 1, band(r), :] = high
            right_lo[stage + 1, band(r), :] = low

            @pl.when(t + reaches[stage] < n_tm)
            def _():
                along(stage, r).start()
        else:
            window_ref[band(r), :] = value
            line = jnp.broadcast_to(weights_ref[pl.ds(r, 1), :], (8, rows))
            occ_ref[...] += jnp.dot(line, value, precision=lax.Precision.HIGHEST,
                                    preferred_element_type=jnp.float32)

    def compute(stage, r):
        if stage == 0:
            full[0, p, band(r), :] = steps_ref[0, band(r), :]
            put(0, r, product(0, r))
        else:
            reach = reaches[stage - 1]

            @pl.when(t >= reach)
            def _():
                put(stage, r, product(stage, r))

            @pl.when(t < reach)
            def _():
                put(stage, r, right_f32[stage - 1, band(r), :])

    def first(r, carry):
        forward(0, r)
        return carry

    lax.fori_loop(0, CHUNKS, first, 0)
    occ_ref[...] = jnp.zeros_like(occ_ref)

    def prepare(r, carry):
        high, low = split(steps_ref[1, band(r), :])
        right_hi[0, band(r), :] = high
        right_lo[0, band(r), :] = low
        return carry

    lax.fori_loop(0, CHUNKS, prepare, 0)

    relay_at = [0, CHUNKS + 1, 2 * CHUNKS + 2]
    forward_at = [None, 3, CHUNKS + 4]

    def step(s, carry):
        def at(begin, do, needs):
            r = s - begin

            @pl.when(jnp.logical_and(jnp.logical_and(r >= 0, r < CHUNKS), needs))
            def _():
                do(r)

        for stage in range(LEVELS + 1):
            needs = t >= (reaches[stage - 1] if stage else 0)
            at(relay_at[stage], functools.partial(relay, stage), needs)
        for stage in range(1, LEVELS + 1):
            at(forward_at[stage], functools.partial(forward, stage), t >= reaches[stage - 1])
        for stage in range(LEVELS + 1):
            at(relay_at[stage] + 1, functools.partial(compute, stage), t >= 0)
        return carry

    lax.fori_loop(0, 3 * CHUNKS + 3, step, 0)

    def drain(r, carry):
        for stage in range(LEVELS + 1):
            @pl.when(t >= (reaches[stage - 1] if stage else 0))
            def _():
                to_partner(stage, r).wait_send()
                for k in range(1, halves):
                    to_other(stage, r, k).wait_send()
                    relayed(stage, r, k).wait_send()
        for stage in range(LEVELS):
            @pl.when(t + reaches[stage] < n_tm)
            def _():
                along(stage, r).wait_send()
        return carry

    lax.fori_loop(0, CHUNKS, drain, 0)


def body(transitions, start_weights):
    _, states, width = transitions.shape
    n_tm, n_panel = lax.axis_size("tm"), lax.axis_size("panel")
    others = n_panel // 2 - 1
    stages = LEVELS + 1
    dma = pltpu.SemaphoreType.DMA
    size = states * width * 4
    window, occupancy = pl.pallas_call(
        functools.partial(kernel, n_tm, n_panel),
        out_shape=(jax.ShapeDtypeStruct((states, width), jnp.float32),
                   jax.ShapeDtypeStruct((8, width), jnp.float32)),
        in_specs=[pl.BlockSpec(memory_space=pltpu.VMEM)] * 2,
        out_specs=[pl.BlockSpec(memory_space=pltpu.VMEM)] * 2,
        scratch_shapes=[
            pltpu.VMEM((stages, n_panel, states, width), jnp.float32),
            pltpu.VMEM((LEVELS, states, width), jnp.float32),
            pltpu.VMEM((stages, states, width), jnp.bfloat16),
            pltpu.VMEM((stages, states, width), jnp.bfloat16),
            dma((stages, CHUNKS)), dma((stages, CHUNKS)),
            dma((stages, others, CHUNKS)), dma((stages, others, CHUNKS)),
            dma((stages, others, CHUNKS)), dma((stages, others, CHUNKS)),
            dma((LEVELS, CHUNKS)), dma((LEVELS, CHUNKS)),
        ],
        compiler_params=pltpu.CompilerParams(
            collective_id=0, has_side_effects=True,
            vmem_limit_bytes=size * (stages * n_panel + 3 * stages + 8)),
    )(transitions, start_weights.reshape(CHUNKS, states // CHUNKS))
    window_kernel = (window * jnp.float32(states))[None]
    return (window_kernel, occupancy[:1])


def solution(mesh):
    placed = (P("tm", None, "panel"), P())
    return jax.shard_map(
        body,
        mesh=mesh,
        in_specs=placed,
        out_specs=(P("tm", None, "panel"), P("tm", "panel")),
        check_vma=False,
    )
```

time: 198 us -> 79.4 us (0.40)
  waiting for transfers between devices: 154 us -> 0 us
  Pallas kernels: 0 us -> 74.7 us
  matrix products: 17.2 us -> 0 us
  between operations: 13.8 us -> 0.65 us
  starting transfers between devices: 6.33 us -> 0 us
    all_gather x3 -> x0, waiting for transfers between devices: 107 us -> none  [the longest x2 70.9 us: body(): lax.all_gather(earlier, 'panel', axis=1, tiled=True)]
    pallas_call x0 -> x1, Pallas kernels: none -> 74.7 us  [body(): pl.pallas_call(functools.partial(kernel, n_tm, n_panel), out_shape=(jax.S...]
    ppermute x2 -> x0, waiting for transfers between devices: 46.6 us -> none  [passed_along(): return lax.ppermute(array, axis, pairs)]
    dot_general x4 -> x0, matrix products: 17.2 us -> none  [matmul_high(): jnp.dot(left, right, precision=lax.Precision.HIGHEST, preferred_element_t...]
    ppermute x2 -> x0, starting transfers between devices: 6.21 us -> none  [passed_along(): return lax.ppermute(array, axis, pairs)]
  transfers between devices with their start and end apart: 5 -> 0, of which waited for: 5 -> 0; matrix products, arithmetic and copies ran while one was open for 0% -> 0% of each run, Pallas kernels for 0% -> 0%
where the time goes in v1:
time: 79.4 us; the launch traced here: 79.3 us
  Pallas kernels  74.7 us (94%)
  local copies, waits for them, and re-layouts  2.83 us (4%)
  other arithmetic  1.04 us (1%)
    pallas_call x1, Pallas kernels, body(): pl.pallas_call(functools.partial(kernel, n_tm, n_panel), out_shape=(jax.S...  74.7 us
    unnamed x4, local copies, waits for them, and re-layouts  2.27 us

profile of v1, /device:TPU:13, one launch (start us, length us, event | category | flops | bytes accessed | tf_op | source)
XLA Modules:
  0.0 79.3 jit_solution(4712434852034903437)
XLA Ops:
  0.6 0.0 copy-start
  0.6 1.6 %copy-done = f32[2,1024,256]{2,1,0:T(8,128)S(1)} copy-done((f32[2,1024,256]{2,1,0:T(8,128)S(1)}, f32[2,1024,256]{2,1,0:T(8,128)}, u32[]{:S(2)}) %copy-start) | copy-done | bytes 2097176
  2.2 0.0 copy-start.1
  2.2 0.7 copy-done.1
  2.9 74.7 %shard_map.41 = (f32[1024,256]{1,0:T(8,128)S(1)}, f32[8,256]{1,0:T(8,128)S(1)}) custom-call(f32[2,1024,256]{2,1,0:T(8,128)S(1)} %copy-done, f32[8,128]{1,0:T(8,128)S(1)} %bitcast.3), custom_call_target="tpu_custom_call" | custom-call | tf_op jit(solution)/shard_map/pallas_call | solution.py:206
  77.7 1.0 %multiply_bitcast_fusion = f32[1,1024,256]{2,1,0:T(8,128)} fusion(f32[1024,256]{1,0:T(8,128)S(1)} %get-tuple-element.4), kind=kLoop, calls=%fused_computation | loop fusion | flops 262144 | bytes 2097152 | tf_op jit(solution)/shard_map/broadcast_in_dim | solution.py:226
  78.7 0.6 slice.3
Async XLA Ops:
  0.6 1.6 %copy-start = (f32[2,1024,256]{2,1,0:T(8,128)S(1)}, f32[2,1024,256]{2,1,0:T(8,128)}, u32[]{:S(2)}) copy-start(f32[2,1024,256]{2,1,0:T(8,128)} %steps_ref.1) | copy-start | bytes 6291460
  2.2 0.7 copy-start.1

commit v2 on v1

--- a/solution.py
+++ b/solution.py
@@ -8,7 +8,7 @@
 from jax.sharding import PartitionSpec as P
 
 LEVELS = 2
-CHUNKS = 8
+CHUNKS = 16
 MESH = pl.DeviceIdType.MESH
 HI = jnp.bfloat16
 
@@ -19,7 +19,7 @@
 
 
 def kernel(n_tm, n_panel, steps_ref, weights_ref, window_ref, occ_ref,
-           full, right_f32, right_hi, right_lo,
+           full, last, right_f32, right_hi, right_lo, fetch,
            lo_send, lo_recv, hi_send, hi_recv, rel_send, rel_recv, tm_send, tm_recv):
     states, width = steps_ref.shape[1:]
     rows = states // CHUNKS
@@ -34,6 +34,11 @@
 
     def back(k):
         return lax.rem(hi + halves - k, halves) * 2 + lo
+
+    first_in = pltpu.make_async_copy(steps_ref.at[0], full.at[0, p], fetch.at[0])
+    last_in = pltpu.make_async_copy(steps_ref.at[1], last, fetch.at[1])
+    last_in.start()
+    first_in.start()
 
     barrier = pltpu.get_barrier_semaphore()
     pl.semaphore_signal(barrier, inc=1, device_id={"panel": partner}, device_id_type=MESH)
@@ -125,11 +130,10 @@
             window_ref[band(r), :] = value
             line = jnp.broadcast_to(weights_ref[pl.ds(r, 1), :], (8, rows))
             occ_ref[...] += jnp.dot(line, value, precision=lax.Precision.HIGHEST,
-                                    preferred_element_type=jnp.float32)
+                                    preferred_element_type=jnp.float32)[:1]
 
     def compute(stage, r):
         if stage == 0:
-            full[0, p, band(r), :] = steps_ref[0, band(r), :]
             put(0, r, product(0, r))
         else:
             reach = reaches[stage - 1]
@@ -148,14 +152,16 @@
 
     lax.fori_loop(0, CHUNKS, first, 0)
     occ_ref[...] = jnp.zeros_like(occ_ref)
+    last_in.wait()
 
     def prepare(r, carry):
-        high, low = split(steps_ref[1, band(r), :])
+        high, low = split(last[band(r), :])
         right_hi[0, band(r), :] = high
         right_lo[0, band(r), :] = low
         return carry
 
     lax.fori_loop(0, CHUNKS, prepare, 0)
+    first_in.wait()
 
     relay_at = [0, CHUNKS + 1, 2 * CHUNKS + 2]
     forward_at = [None, 3, CHUNKS + 4]
@@ -206,14 +212,16 @@
     window, occupancy = pl.pallas_call(
         functools.partial(kernel, n_tm, n_panel),
         out_shape=(jax.ShapeDtypeStruct((states, width), jnp.float32),
-                   jax.ShapeDtypeStruct((8, width), jnp.float32)),
-        in_specs=[pl.BlockSpec(memory_space=pltpu.VMEM)] * 2,
+                   jax.ShapeDtypeStruct((1, width), jnp.float32)),
+        in_specs=[pl.BlockSpec(memory_space=pltpu.HBM), pl.BlockSpec(memory_space=pltpu.VMEM)],
         out_specs=[pl.BlockSpec(memory_space=pltpu.VMEM)] * 2,
         scratch_shapes=[
             pltpu.VMEM((stages, n_panel, states, width), jnp.float32),
+            pltpu.VMEM((states, width), jnp.float32),
             pltpu.VMEM((LEVELS, states, width), jnp.float32),
             pltpu.VMEM((stages, states, width), jnp.bfloat16),
             pltpu.VMEM((stages, states, width), jnp.bfloat16),
+            dma((2,)),
             dma((stages, CHUNKS)), dma((stages, CHUNKS)),
             dma((stages, others, CHUNKS)), dma((stages, others, CHUNKS)),
             dma((stages, others, CHUNKS)), dma((stages, others, CHUNKS)),
@@ -224,7 +232,7 @@
             vmem_limit_bytes=size * (stages * n_panel + 3 * stages + 8)),
     )(transitions, start_weights.reshape(CHUNKS, states // CHUNKS))
     window_kernel = (window * jnp.float32(states))[None]
-    return (window_kernel, occupancy[:1])
+    return (window_kernel, occupancy)
 
 
 def solution(mesh):

time: 79.4 us -> 81.2 us (1.023)
  Pallas kernels: 74.7 us -> 76.4 us
    pallas_call x1, Pallas kernels: 74.7 us -> 76.4 us  [body(): pl.pallas_call(functools.partial(kernel, n_tm, n_panel), out_shape=(jax.S...]
    unnamed x4 -> x3, local copies, waits for them, and re-layouts: 2.27 us -> 2.15 us
where the time goes in v2:
time: 81.2 us; the launch traced here: 81 us
  Pallas kernels  76.4 us (94%)
  local copies, waits for them, and re-layouts  2.91 us (4%)
  other arithmetic  1.04 us (1%)
    pallas_call x1, Pallas kernels, body(): pl.pallas_call(functools.partial(kernel, n_tm, n_panel), out_shape=(jax.S...  76.4 us
    unnamed x3, local copies, waits for them, and re-layouts  2.15 us

profile of v2, /device:TPU:13, one launch (start us, length us, event | category | flops | bytes accessed | tf_op | source)
XLA Modules:
  0.0 81.0 jit_solution(11520678268333771944)
XLA Ops:
  0.6 0.8 reshape.7.weights_ref
  1.4 0.0 copy-start
  1.4 1.6 %copy-done = f32[2,1024,256]{2,1,0:T(8,128)S(1)} copy-done((f32[2,1024,256]{2,1,0:T(8,128)S(1)}, f32[2,1024,256]{2,1,0:T(8,128)}, u32[]{:S(2)}) %copy-start) | copy-done | bytes 2097176
  3.0 76.4 %shard_map.41 = (f32[1024,256]{1,0:T(8,128)S(1)}, f32[1,256]{1,0:T(1,128)S(1)}) custom-call(f32[2,1024,256]{2,1,0:T(8,128)S(1)} %copy-done, f32[16,64]{1,0:T(8,128)S(1)} %reshape.7.weights_ref), custom_call_target="tpu_custom_call" | custom-call | tf_op jit(solution)/shard_map/pallas_call | solution.py:212
  79.4 1.0 %multiply_bitcast_fusion = f32[1,1024,256]{2,1,0:T(8,128)} fusion(f32[1024,256]{1,0:T(8,128)S(1)} %get-tuple-element.4), kind=kLoop, calls=%fused_computation | loop fusion | flops 262144 | bytes 2097152 | tf_op jit(solution)/shard_map/broadcast_in_dim | solution.py:234
  80.4 0.6 copy.5
Async XLA Ops:
  1.4 1.6 %copy-start = (f32[2,1024,256]{2,1,0:T(8,128)S(1)}, f32[2,1024,256]{2,1,0:T(8,128)}, u32[]{:S(2)}) copy-start(f32[2,1024,256]{2,1,0:T(8,128)} %steps_ref.1) | copy-start | bytes 6291460

commit v3 on v1

--- a/solution.py
+++ b/solution.py
@@ -122,7 +122,7 @@
             def _():
                 along(stage, r).start()
         else:
-            window_ref[band(r), :] = value
+            window_ref[band(r), :] = value * jnp.float32(states)
             line = jnp.broadcast_to(weights_ref[pl.ds(r, 1), :], (8, rows))
             occ_ref[...] += jnp.dot(line, value, precision=lax.Precision.HIGHEST,
                                     preferred_element_type=jnp.float32)
@@ -223,7 +223,7 @@
             collective_id=0, has_side_effects=True,
             vmem_limit_bytes=size * (stages * n_panel + 3 * stages + 8)),
     )(transitions, start_weights.reshape(CHUNKS, states // CHUNKS))
-    window_kernel = (window * jnp.float32(states))[None]
+    window_kernel = window[None]
     return (window_kernel, occupancy[:1])
 
 

time: 79.4 us -> 79.4 us (level)
  other arithmetic: 1.04 us -> 0 us
  local copies, waits for them, and re-layouts: 2.83 us -> 3.8 us
    broadcast_in_dim x1 -> x0, other arithmetic: 1.04 us -> none  [body(): window_kernel = (window * jnp.float32(states))[None]]
    unnamed x4 -> x5, local copies, waits for them, and re-layouts: 2.27 us -> 3.24 us
where the time goes in v3:
time: 79.4 us; the launch traced here: 79.2 us
  Pallas kernels  74.7 us (94%)
  local copies, waits for them, and re-layouts  3.8 us (5%)
    pallas_call x1, Pallas kernels, body(): pl.pallas_call(functools.partial(kernel, n_tm, n_panel), out_shape=(jax.S...  74.7 us
    unnamed x5, local copies, waits for them, and re-layouts  3.24 us

profile of v3, /device:TPU:13, one launch (start us, length us, event | category | flops | bytes accessed | tf_op | source)
XLA Modules:
  0.0 79.2 jit_solution(13361147388653432665)
XLA Ops:
  0.6 0.0 copy-start
  0.6 1.6 %copy-done = f32[2,1024,256]{2,1,0:T(8,128)S(1)} copy-done((f32[2,1024,256]{2,1,0:T(8,128)S(1)}, f32[2,1024,256]{2,1,0:T(8,128)}, u32[]{:S(2)}) %copy-start) | copy-done | bytes 2097176
  2.2 0.0 copy-start.1
  2.2 0.7 copy-done.1
  2.9 74.7 %shard_map.41 = (f32[1024,256]{1,0:T(8,128)S(1)}, f32[8,256]{1,0:T(8,128)S(1)}) custom-call(f32[2,1024,256]{2,1,0:T(8,128)S(1)} %copy-done, f32[8,128]{1,0:T(8,128)S(1)} %bitcast.3), custom_call_target="tpu_custom_call" | custom-call | tf_op jit(solution)/shard_map/pallas_call | solution.py:206
  77.7 0.6 slice.3
  78.2 1.0 %copy.5 = f32[1,1024,256]{2,1,0:T(8,128)} copy(f32[1,1024,256]{2,1,0:T(8,128)S(1)} %bitcast.2) | data formatting | bytes 2097152
Async XLA Ops:
  0.6 1.6 %copy-start = (f32[2,1024,256]{2,1,0:T(8,128)S(1)}, f32[2,1024,256]{2,1,0:T(8,128)}, u32[]{:S(2)}) copy-start(f32[2,1024,256]{2,1,0:T(8,128)} %steps_ref.1) | copy-start | bytes 6291460
  2.2 0.7 copy-start.1

commit v4 on v3

--- a/solution.py
+++ b/solution.py
@@ -125,7 +125,7 @@
             window_ref[band(r), :] = value * jnp.float32(states)
             line = jnp.broadcast_to(weights_ref[pl.ds(r, 1), :], (8, rows))
             occ_ref[...] += jnp.dot(line, value, precision=lax.Precision.HIGHEST,
-                                    preferred_element_type=jnp.float32)
+                                    preferred_element_type=jnp.float32)[:1]
 
     def compute(stage, r):
         if stage == 0:
@@ -143,10 +143,16 @@
                 put(stage, r, right_f32[stage - 1, band(r), :])
 
     def first(r, carry):
-        forward(0, r)
+        for k in range(1, halves):
+            to_other(0, r, k).start()
+        return carry
+
+    def first_partner(r, carry):
+        to_partner(0, r).start()
         return carry
 
     lax.fori_loop(0, CHUNKS, first, 0)
+    lax.fori_loop(0, CHUNKS, first_partner, 0)
     occ_ref[...] = jnp.zeros_like(occ_ref)
 
     def prepare(r, carry):
@@ -206,7 +212,7 @@
     window, occupancy = pl.pallas_call(
         functools.partial(kernel, n_tm, n_panel),
         out_shape=(jax.ShapeDtypeStruct((states, width), jnp.float32),
-                   jax.ShapeDtypeStruct((8, width), jnp.float32)),
+                   jax.ShapeDtypeStruct((1, width), jnp.float32)),
         in_specs=[pl.BlockSpec(memory_space=pltpu.VMEM)] * 2,
         out_specs=[pl.BlockSpec(memory_space=pltpu.VMEM)] * 2,
         scratch_shapes=[
@@ -224,7 +230,7 @@
             vmem_limit_bytes=size * (stages * n_panel + 3 * stages + 8)),
     )(transitions, start_weights.reshape(CHUNKS, states // CHUNKS))
     window_kernel = window[None]
-    return (window_kernel, occupancy[:1])
+    return (window_kernel, occupancy)
 
 
 def solution(mesh):

time: 79.4 us -> 79.4 us (level)
    unnamed x5 -> x6, local copies, waits for them, and re-layouts: 3.24 us -> 3.8 us
where the time goes in v4:
time: 79.4 us; the launch traced here: 79.2 us
  Pallas kernels  74.7 us (94%)
  local copies, waits for them, and re-layouts  3.8 us (5%)
    pallas_call x1, Pallas kernels, body(): pl.pallas_call(functools.partial(kernel, n_tm, n_panel), out_shape=(jax.S...  74.7 us
    unnamed x6, local copies, waits for them, and re-layouts  3.8 us

profile of v4, /device:TPU:13, one launch (start us, length us, event | category | flops | bytes accessed | tf_op | source)
XLA Modules:
  0.0 79.2 jit_solution(17123292619137054894)
XLA Ops:
  0.6 0.0 copy-start
  0.6 1.6 %copy-done = f32[2,1024,256]{2,1,0:T(8,128)S(1)} copy-done((f32[2,1024,256]{2,1,0:T(8,128)S(1)}, f32[2,1024,256]{2,1,0:T(8,128)}, u32[]{:S(2)}) %copy-start) | copy-done | bytes 2097176
  2.2 0.0 copy-start.1
  2.2 0.7 copy-done.1
  2.9 74.7 %shard_map.41 = (f32[1024,256]{1,0:T(8,128)S(1)}, f32[1,256]{1,0:T(1,128)S(1)}) custom-call(f32[2,1024,256]{2,1,0:T(8,128)S(1)} %copy-done, f32[8,128]{1,0:T(8,128)S(1)} %bitcast.3), custom_call_target="tpu_custom_call" | custom-call | tf_op jit(solution)/shard_map/pallas_call | solution.py:212
  77.7 1.0 %copy.6 = f32[1,1024,256]{2,1,0:T(8,128)} copy(f32[1,1024,256]{2,1,0:T(8,128)S(1)} %bitcast.2) | data formatting | bytes 2097152
  78.6 0.6 copy.7
Async XLA Ops:
  0.6 1.6 %copy-start = (f32[2,1024,256]{2,1,0:T(8,128)S(1)}, f32[2,1024,256]{2,1,0:T(8,128)}, u32[]{:S(2)}) copy-start(f32[2,1024,256]{2,1,0:T(8,128)} %steps_ref.1) | copy-start | bytes 6291460
  2.2 0.7 copy-start.1
